TPU v7x, 256 devices: a whole 4x4x8 slice. The times are simulated.
256 devices in a mesh: grp: 4 (over x), wide: 64 (over y, z, core).
Axes of the slice: x: 4, y: 4, z: 8, core: 2. Of those that a mesh axis runs over, the one named last changes fastest.
Arguments:
- embeddings: float32 [393216, 768], P(('grp', 'wide')), may hold values from -200 to 200, as said below
Outputs:
- whitened: float32 [393216, 768], P(('grp', 'wide'))
- factor_scaled: float32 [768, 768], replicated
Inputs may be any that keep to these rules, and one draw needn't show every extreme that they name: `embeddings`: Real-valued rows; no structure is promised.
All inputs are finite; a program needn't handle non-finite values.
Results may differ from a plain program's by a relative error of at most 0.000054.
Values sent between devices are 32-bit elements; how exact they have to be, the bound alone decides.
A program may use at most 128 MiB of HBM per device.

v0:
```python
import jax
import jax.numpy as jnp
from jax import lax
from jax.sharding import PartitionSpec as P


def self_product(rows):
    return lax.dot_general(
        rows,
        rows,
        (((0,), (0,)), ((), ())),
        precision=lax.Precision.HIGHEST,
        preferred_element_type=jnp.float32,
    )


def shards(embeddings):
    row_count = embeddings.shape[0] * lax.axis_size("grp") * lax.axis_size("wide")
    col_total = lax.psum(jnp.sum(embeddings, axis=0), ("grp", "wide"))
    col_mean = col_total / row_count
    centred = embeddings - col_mean[None, :]
    payload = lax.psum(self_product(centred), ("grp", "wide"))
    lower = jnp.linalg.cholesky(payload)
    factor = lower.T
    scale = jnp.sqrt(jnp.float32(row_count))
    solved = jax.scipy.linalg.solve_triangular(lower, centred.T, lower=True)
    whitened = solved.T * scale
    return (whitened, factor / scale)


def solution(mesh):
    placed = (P(("grp", "wide"), None),)
    return jax.shard_map(
        shards,
        mesh=mesh,
        in_specs=placed,
        out_specs=(P(("grp", "wide"), None), P()),
        check_vma=False,
    )
```

profile of v0, /device:TPU:1, one launch (start us, length us, event | category | flops | bytes accessed | tf_op | source)
XLA Modules:
  0.0 636.5 jit_solution(5959978019660776610)
XLA Ops:
  7.2 2.7 reduce_sum.9
  9.9 81.4 %psum.14 = f32[768]{0:T(1024)S(1)} all-reduce(f32[768]{0:T(1024)S(1)} %reduce_sum.9), channel_id=1, replica_groups=mesh['grp'=4,'wide'=64] {'grp','wide'}, use_global_device_ids=true, to_apply=%region_1.0 | all-reduce | flops 768 | bytes 6144 | tf_op jit(solution)/shard_map/psum | solution.py:19
  91.3 16.3 %fusion = f32[768,768]{0,1:T(8,128)} fusion(f32[1536,768]{1,0:T(8,128)} %param.1, f32[768]{0:T(1024)S(1)} %broadcast_multiply_fusion), kind=kOutput, calls=%fused_computation.4 | convolution fusion | flops 10872815616 | bytes 7080960 | tf_op jit(solution)/shard_map/dot_general | solution.py:8
  107.7 4.8 subtract_bitcast_fusion
  112.5 250.3 %all-reduce.3.cloned.1.call-done = f32[768,768]{0,1:T(8,128)} async-done(((f32[768,768]{0,1:T(8,128)}), f32[768,768]{0,1:T(8,128)}) %all-reduce.3.cloned.1.call-update) | async-done | bytes 2359312 | tf_op jit(solution)/shard_map/psum | solution.py:22
  362.8 3.6 copy.4
  369.9 11.7 %cholesky.165 = f32[128,128]{1,0:T(8,128)S(1)} custom-call(f32[128,128]{1,0:T(8,128)S(1)} %cholesky.424), custom_call_target="Cholesky" | custom-call | tf_op jit(solution)/shard_map/jit(cholesky)/cholesky | solution.py:23
  381.8 9.8 %custom-call.47 = f32[1,128,128]{1,2,0:T(8,128)S(1)} custom-call(f32[1,128,128]{2,1,0:T(8,128)S(1)} %get-tuple-element.49), custom_call_target="InvertDiagBlocksLowerTriangular" | custom-call | tf_op jit(solution)/shard_map/jit(cholesky)/cholesky | solution.py:23
  394.4 11.7 %cholesky.188 = f32[128,128]{1,0:T(8,128)S(1)} custom-call(f32[128,128]{1,0:T(8,128)S(1)} %cholesky.428), custom_call_target="Cholesky" | custom-call | tf_op jit(solution)/shard_map/jit(cholesky)/cholesky | solution.py:23
  406.2 10.0 %custom-call.48 = f32[1,128,128]{1,2,0:T(8,128)S(1)} custom-call(f32[1,128,128]{2,1,0:T(8,128)S(1)} %get-tuple-element.46), custom_call_target="InvertDiagBlocksLowerTriangular" | custom-call | tf_op jit(solution)/shard_map/jit(cholesky)/cholesky | solution.py:23
  418.0 11.7 %cholesky.354 = f32[128,128]{1,0:T(8,128)S(1)} custom-call(f32[128,128]{1,0:T(8,128)S(1)} %cholesky.433), custom_call_target="Cholesky" | custom-call | tf_op jit(solution)/shard_map/jit(cholesky)/cholesky | solution.py:23
  430.5 9.8 %custom-call.49 = f32[1,128,128]{1,2,0:T(8,128)S(1)} custom-call(f32[1,128,128]{2,1,0:T(8,128)S(1)} %get-tuple-element.43), custom_call_target="InvertDiagBlocksLowerTriangular" | custom-call | tf_op jit(solution)/shard_map/jit(cholesky)/cholesky | solution.py:23
  442.2 12.1 %cholesky.373 = f32[128,128]{1,0:T(8,128)S(1)} custom-call(f32[128,128]{1,0:T(8,128)S(1)} %cholesky.438), custom_call_target="Cholesky" | custom-call | tf_op jit(solution)/shard_map/jit(cholesky)/cholesky | solution.py:23
  455.0 9.8 %custom-call.50 = f32[1,128,128]{1,2,0:T(8,128)S(1)} custom-call(f32[1,128,128]{2,1,0:T(8,128)S(1)} %get-tuple-element.40), custom_call_target="InvertDiagBlocksLowerTriangular" | custom-call | tf_op jit(solution)/shard_map/jit(cholesky)/cholesky | solution.py:23
  466.6 11.7 %cholesky.392 = f32[128,128]{1,0:T(8,128)S(1)} custom-call(f32[128,128]{1,0:T(8,128)S(1)} %cholesky.443), custom_call_target="Cholesky" | custom-call | tf_op jit(solution)/shard_map/jit(cholesky)/cholesky | solution.py:23
  479.0 9.8 %custom-call.51 = f32[1,128,128]{1,2,0:T(8,128)S(1)} custom-call(f32[1,128,128]{2,1,0:T(8,128)S(1)} %get-tuple-element.37), custom_call_target="InvertDiagBlocksLowerTriangular" | custom-call | tf_op jit(solution)/shard_map/jit(cholesky)/cholesky | solution.py:23
  490.3 11.9 %cholesky.410 = f32[128,128]{1,0:T(8,128)S(1)} custom-call(f32[128,128]{1,0:T(8,128)S(1)} %convolution_subtract_fusion.8), custom_call_target="Cholesky" | custom-call | tf_op jit(solution)/shard_map/jit(cholesky)/cholesky | solution.py:23
  507.4 2.5 multiply_bitcast_fusion.1
  509.9 3.1 copy.6
  513.0 16.7 %while.1 = (s32[]{:T(128)}, f32[768,768]{1,0:T(8,128)}, s32[6,2]{0,1:T(2,128)S(1)}, f32[6,128,128]{2,1,0:T(8,128)S(1)}, s32[]{:T(128)}) while((s32[]{:T(128)}, f32[768,768]{1,0:T(8,128)}, s32[6,2]{0,1:T(2,128)S(1)}, f32[6,128,128]{2,1,0:T(8,128)S(1)}, s32[]{:T(128)}) %tuple.46), condition=%wide.while_cond, body=%wide.while_body.sunk | while | flops 2 | bytes 131189 | solution.py:26
  513.6 2.2 bitcast_dynamic-update-slice_fusion.2
  516.4 2.2 bitcast_dynamic-update-slice_fusion.2
  519.2 2.2 bitcast_dynamic-update-slice_fusion.2
  522.0 2.2 bitcast_dynamic-update-slice_fusion.2
  529.7 59.0 %custom-call.52 = f32[6,128,128]{1,2,0:T(8,128)S(1)} custom-call(f32[6,128,128]{2,1,0:T(8,128)S(1)} %get-tuple-element.9), custom_call_target="InvertDiagBlocksLowerTriangular" | custom-call | tf_op jit(solution)/shard_map/jit(_solve_triangular)/triangular_solve | solution.py:26
  590.9 2.6 convolution_subtract_fusion.3
  594.4 3.6 convolution_subtract_fusion
  599.0 5.0 convolution_subtract_fusion.2
  604.9 6.4 %fusion.10 = f32[128,1536]{0,1:T(8,128)S(1)} fusion(f32[128,1536]{1,0:T(8,128)S(1)} %get-tuple-element.55, f32[128,1536]{1,0:T(8,128)S(1)} %get-tuple-element.54, f32[128,1536]{1,0:T(8,128)S(1)} %get-tuple-element.53, f32[128,1536]{1,0:T(8,128)S(1)} %get-tuple-element.52, f32[768,1536]{0,1:T(8,128)S(1)} %bitcast.84, f32[768,768]{1,0:T(8,128)} %get-tuple-element.104), kind=kOutput, calls=%fused_computation.19 | convolution fusion | flops 1210515456 | bytes 4980736 | tf_op jit(solution)/shard_map/jit(_solve_triangular)/triangular_solve | solution.py:26
  612.2 7.5 %convolution_subtract_fusion.1 = f32[128,1536]{0,1:T(8,128)S(1)} fusion(f32[640,1536]{1,0:T(8,128)S(1)} %get-tuple-element.24, f32[768,1536]{0,1:T(8,128)S(1)} %bitcast.84, f32[768,768]{1,0:T(8,128)} %get-tuple-element.104), kind=kOutput, calls=%fused_computation.16 | convolution fusion | flops 1510146048 | bytes 5832704 | tf_op jit(solution)/shard_map/jit(_solve_triangular)/triangular_solve | solution.py:26
  620.6 2.6 multiply_bitcast_fusion
  623.2 6.0 copy.5
  (63 shorter events, 31.6 us)
Async XLA Ops:
  7.2 355.7 %all-reduce.3.cloned.1.call-start = ((), (), s32[]{:S(2)}) async-start(), calls=%async_computation | async-start | bytes 4718592 | tf_op jit(solution)/shard_map/psum | solution.py:22
  362.8 3.6 copy-start
  368.5 1.4 copy-start.1
  509.9 84.5 %slice-start = ((s8[4718592]{0:T(1024)(128)(4,1)}), s8[524288]{0:T(1024)(128)(4,1)S(1)}, s32[]{:S(2)}) async-start(s8[4718592]{0:T(1024)(128)(4,1)} %bitcast.83), calls=%async_computation.1 | async-start | bytes 1048576
  588.7 5.7 slice-start.1
Sparse Core Ops, SparseCore 0:
  107.8 255.0 all-reduce.2
where the time goes:
time: 644 us; the launch traced here: 636 us
  waiting for transfers between devices  250 us (39%)
  other arithmetic  197 us (31%)
  blocking collectives  81.4 us (13%)
  matrix products  57.9 us (9%)
  local copies, waits for them, and re-layouts  31 us (5%)
  between operations  18.5 us (3%)
    psum x1, waiting for transfers between devices, shards(): payload = lax.psum(self_product(centred), ('grp', 'wide'))  250 us
    another operation x22, other arithmetic, shards(): lower = jnp.linalg.cholesky(payload)  124 us
    psum x1, blocking collectives, shards(): col_total = lax.psum(jnp.sum(embeddings, axis=0), ('grp', 'wide'))  81.4 us
    another operation x2, other arithmetic, shards(): solved = jax.scipy.linalg.solve_triangular(lower, centred.T, lower=True)  59 us
    another operation x11, matrix products, shards(): solved = jax.scipy.linalg.solve_triangular(lower, centred.T, lower=True)  31.8 us
    another operation x18, local copies, waits for them, and re-layouts  16.6 us
    dot_general x1, matrix products, self_product(): lax.dot_general(rows, rows, (((0,), (0,)), ((), ())), precision=lax.Preci...  16.3 us
  transfers between devices with their start and end apart: 1, of which 1 were waited for; matrix products, arithmetic and copies ran while one was open for 1% of the time, Pallas kernels for 0%

commit v1 on v0

v1 whole, which is shorter than its diff:
```python
import functools
import math

import jax
import jax.numpy as jnp
from jax import lax
from jax.experimental import pallas as pl
from jax.experimental.pallas import tpu as pltpu
from jax.sharding import PartitionSpec as P

F32 = jnp.float32
BF16 = jnp.bfloat16
HI = lax.Precision.HIGHEST
MESH = pl.DeviceIdType.MESH
B = 128
TT = (((0,), (0,)), ((), ()))
NT = (((1,), (1,)), ((), ()))


def tri_blocks(nb):
    return [(i, j) for i in range(nb) for j in range(i, nb)]


def split(x):
    hi = x.astype(BF16)
    return hi, (x - hi.astype(F32)).astype(BF16)


def gram_kernel(
    dims,
    x_ref,
    g_ref,
    mean_ref,
    hi,
    lo,
    own,
    from_core,
    a_in,
    b_own,
    b_in,
    z_own,
    z_in,
    z_all,
    b_all,
    mbuf,
    m_in,
    ssem,
    rsem,
):
    nx, ny, nz, width = dims
    rows = x_ref.shape[0]
    nb = width // B
    blocks = tri_blocks(nb)
    at = {ij: k for k, ij in enumerate(blocks)}

    mx = lax.axis_index("grp")
    wide = lax.axis_index("wide")
    mc = lax.rem(wide, 2)
    chip = wide // 2
    mz = lax.rem(chip, nz)
    my = chip // nz

    def dev(x, y, z, c):
        return (x, (y * nz + z) * 2 + c)

    def x_peer(d):
        return dev(lax.rem(mx + d, nx), my, mz, mc)

    def y_peer(d):
        return dev(mx, lax.rem(my + d, ny), mz, mc)

    def z_peer(d):
        return dev(mx, my, lax.rem(mz + d, nz), mc)

    core_peer = dev(mx, my, mz, 1 - mc)
    everyone = (
        [core_peer]
        + [x_peer(d) for d in range(1, nx)]
        + [y_peer(d) for d in range(1, ny)]
        + [z_peer(d) for d in range(1, nz)]
    )
    barrier = pltpu.get_barrier_semaphore()
    for who in everyone:
        pl.semaphore_signal(barrier, inc=1, device_id=who, device_id_type=MESH)

    counter = [0]

    def send(src, dst, who):
        k = counter[0]
        counter[0] += 1
        copy = pltpu.make_async_remote_copy(
            src_ref=src,
            dst_ref=dst,
            send_sem=ssem.at[k],
            recv_sem=rsem.at[k],
            device_id=who,
            device_id_type=MESH,
        )
        copy.start()
        sent.append(copy)
        return copy

    sent = []

    total = jnp.sum(x_ref[...], axis=0, keepdims=True)
    local = total * (1.0 / rows)
    mbuf[0] = jnp.zeros((8, B), F32)
    for i in range(nb):
        mbuf[0, i : i + 1, :] = local[:, i * B : (i + 1) * B]

    pl.semaphore_wait(barrier, len(everyone))

    def mean_phase(stage, peers, base):
        copies = [
            send(mbuf.at[stage], m_in.at[base + d], who) for d, who in enumerate(peers)
        ]

        def finish():
            acc = mbuf[stage]
            for d, copy in enumerate(copies):
                copy.wait_recv()
                acc = acc + m_in[base + d]
            mbuf[stage + 1] = acc

        return finish

    stages = [
        [core_peer],
        [x_peer(d) for d in range(1, nx)],
        [y_peer(d) for d in range(1, ny)],
        [z_peer(d) for d in range(1, nz)],
    ]
    base = 0
    finish = mean_phase(0, stages[0], base)
    base += 1
    centred = x_ref[...] - local
    h, l = split(centred)
    hi[...] = h
    lo[...] = l

    for part in range(3):
        finish()
        finish = mean_phase(part + 1, stages[part + 1], base)
        base += len(stages[part + 1])
        top = 2 * B * (part + 1)
        cols = slice(2 * B * part, top)
        g = lax.dot_general(hi[:, :top], hi[:, cols], TT, preferred_element_type=F32)
        g += lax.dot_general(hi[:, :top], lo[:, cols], TT, preferred_element_type=F32)
        g += lax.dot_general(lo[:, :top], hi[:, cols], TT, preferred_element_type=F32)
        g += lax.dot_general(lo[:, :top], lo[:, cols], TT, preferred_element_type=F32)
        for j in (2 * part, 2 * part + 1):
            for i in range(j + 1):
                off = (j - 2 * part) * B
                own[at[i, j]] = g[i * B : (i + 1) * B, off : off + B]
    finish()
    count = nx * ny * nz * 2
    mean8 = mbuf[4] * (1.0 / count)
    for i in range(nb):
        mean_ref[:, i * B : (i + 1) * B] = mean8[i : i + 1, :]
    delta = mbuf[0] - mean8
    delta_t = delta.T * float(rows)
    for i in range(nb):
        col = jnp.broadcast_to(delta_t[:, i : i + 1], (B, B))
        for j in range(i, nb):
            row = jnp.broadcast_to(delta[j : j + 1, :], (B, B))
            own[at[i, j]] = own[at[i, j]] + col * row

    own_t = own.reshape(2, 2, nx, -1, B)
    core_t = from_core.reshape(2, nx, -1, B)
    ta = own_t.shape[3]
    g_t = g_ref.reshape(2, 2, nx, ta, B)
    tb = b_in.shape[2]

    core_copies = [
        [
            send(own_t.at[1 - mc, q, k], core_t.at[q, k], core_peer)
            for q in range(2)
        ]
        for k in range(nx)
    ]
    core_copies = [[core_copies[k][q] for k in range(nx)] for q in range(2)]
    ax = [(x_peer, mx), (y_peer, my)]
    a_copies = [[], []]
    for c in core_copies[0] + core_copies[1]:
        c.wait_recv()
    for d in list(range(1, nx)) + [0]:
        for q in range(2):
            peer, me = ax[q]
            k = lax.rem(me + d, nx)
            own_t[mc, q, k] = own_t[mc, q, k] + core_t[q, k]
            if d:
                a_copies[q].append(send(own_t.at[mc, q, k], a_in.at[q, d - 1], peer(d)))
    b_copies = [[], []]
    for q in range(2):
        me = ax[q][1]
        acc = own_t[mc, q, me]
        for d in range(1, nx):
            a_copies[q][d - 1].wait_recv()
            acc = acc + a_in[q, d - 1]
        b_own[q, 0:ta] = acc
        b_own[q, ta:] = jnp.zeros((b_own.shape[1] - ta, B), F32)
        peer, me = ax[1 - q]
        for d in range(1, ny):
            k = lax.rem(me + d, ny)
            b_copies[q].append(
                send(
                    b_own.at[q, pl.ds(pl.multiple_of(k * tb, 8), tb)],
                    b_in.at[q, d - 1],
                    peer(d),
                )
            )
    for q in range(2):
        me = ax[1 - q][1]
        acc = b_own[q, pl.ds(pl.multiple_of(me * tb, 8), tb)]
        for d in range(1, ny):
            b_copies[q][d - 1].wait_recv()
            acc = acc + b_in[q, d - 1]
        z_own[q * tb : (q + 1) * tb] = acc
    tz = z_in.shape[1]
    z_own[2 * tb :] = jnp.zeros((z_own.shape[0] - 2 * tb, B), F32)
    z_copies = []
    for d in range(1, nz):
        k = lax.rem(mz + d, nz)
        z_copies.append(
            send(z_own.at[pl.ds(pl.multiple_of(k * tz, 8), tz)], z_in.at[d - 1], z_peer(d))
        )
    acc = z_own[pl.ds(pl.multiple_of(mz * tz, 8), tz)]
    for d in range(1, nz):
        z_copies[d - 1].wait_recv()
        acc = acc + z_in[d - 1]
    mine = pl.ds(pl.multiple_of(mz * tz, 8), tz)
    z_all[mine] = acc
    z_copies = [send(z_all.at[mine], z_all.at[mine], z_peer(d)) for d in range(1, nz)]
    for c in z_copies:
        c.wait_recv()
    b_copies = [[], []]
    for q in range(2):
        peer, me = ax[1 - q]
        mine = pl.ds(pl.multiple_of(me * tb, 8), tb)
        src = z_all.at[q * tb : (q + 1) * tb]
        b_copies[q] = [send(src, b_all.at[q, mine], peer(d)) for d in range(1, ny)]
        b_all[q, mine] = z_all[q * tb : (q + 1) * tb]
    a_copies = [[], []]
    core_copies = []
    for q in range(2):
        for c in b_copies[q]:
            c.wait_recv()
        peer, me = ax[q]
        src = b_all.at[q, 0:ta]
        a_copies[q] = [send(src, g_t.at[mc, q, me], peer(d)) for d in range(1, nx)]
        core_copies.append(send(src, g_t.at[mc, q, me], core_peer))
        g_t[mc, q, me] = b_all[q, 0:ta]
    for d in range(1, nx):
        for q in range(2):
            a_copies[q][d - 1].wait_recv()
            k = lax.rem(ax[q][1] + nx - d, nx)
            core_copies.append(send(g_t.at[mc, q, k], g_t.at[mc, q, k], core_peer))
    for c in core_copies:
        c.wait_recv()
    for c in sent:
        c.wait_send()


def summed_gram(dims, x):
    nx, ny, nz, width = dims
    rows = x.shape[0]
    nb = width // B
    n_blocks = nb * (nb + 1) // 2
    total = n_blocks * B
    ta = total // (4 * nx)
    tb = -(-ta // (8 * ny)) * 8
    tz = -(-2 * tb // (8 * nz)) * 8
    n_mean = 1 + (nx - 1) + (ny - 1) + (nz - 1)
    n_copies = n_mean + 2 * (2 * nx + 2 * (nx - 1) + 2 * (ny - 1) + nz - 1)
    vmem = pl.BlockSpec(memory_space=pltpu.VMEM)
    return pl.pallas_call(
        functools.partial(gram_kernel, dims),
        out_shape=(
            jax.ShapeDtypeStruct((n_blocks, B, B), F32),
            jax.ShapeDtypeStruct((1, width), F32),
        ),
        in_specs=[vmem],
        out_specs=(vmem, vmem),
        scratch_shapes=[
            pltpu.VMEM((rows, width), BF16),
            pltpu.VMEM((rows, width), BF16),
            pltpu.VMEM((n_blocks, B, B), F32),
            pltpu.VMEM((total // 2, B), F32),
            pltpu.VMEM((2, nx - 1, ta, B), F32),
            pltpu.VMEM((2, tb * ny, B), F32),
            pltpu.VMEM((2, ny - 1, tb, B), F32),
            pltpu.VMEM((tz * nz, B), F32),
            pltpu.VMEM((nz - 1, tz, B), F32),
            pltpu.VMEM((tz * nz, B), F32),
            pltpu.VMEM((2, tb * ny, B), F32),
            pltpu.VMEM((5, 8, B), F32),
            pltpu.VMEM((n_mean, 8, B), F32),
            pltpu.SemaphoreType.DMA((n_copies,)),
            pltpu.SemaphoreType.DMA((n_copies,)),
        ],
        compiler_params=pltpu.CompilerParams(
            collective_id=0, has_side_effects=True, vmem_limit_bytes=56 << 20
        ),
        cost_estimate=pl.CostEstimate(
            flops=2 * rows * width * width, bytes_accessed=4 * rows * width, transcendentals=0
        ),
        name="summed_gram",
    )(x)


def rows_bcast(x, k):
    return jnp.broadcast_to(x[k : k + 1, :], (8, B))


def lane_bcast(x, c):
    return jnp.broadcast_to(x[:, c : c + 1], (8, B))


def factor_block(S):
    lane = lax.broadcasted_iota(jnp.int32, (8, B), 1)
    sub = lax.broadcasted_iota(jnp.int32, (8, B), 0)
    S = list(S)
    out = []
    for p in range(16):
        base = 8 * p
        inpanel = (lane >= base) & (lane < base + 8)
        cols = [lane_bcast(S[p], base + j) for j in range(8)]
        D = {(k, j): rows_bcast(cols[j], k) for j in range(8) for k in range(j + 1)}
        row = [
            jnp.where(inpanel, jnp.where(lane == base + k, 1.0, 0.0), rows_bcast(S[p], k))
            for k in range(8)
        ]
        m = {}
        r = [None] * 8
        for j in range(8):
            r[j] = 1.0 / D[j, j]
            for k in range(j + 1, 8):
                m[j, k] = D[j, k] * r[j]
                for l in range(k, 8):
                    D[k, l] = D[k, l] - m[j, k] * D[j, l]
                row[k] = row[k] - m[j, k] * row[j]
        rs = [lax.rsqrt(D[j, j]) for j in range(8)]
        v = [row[j] * r[j] for j in range(8)]
        q = list(v)
        for k in range(6, -1, -1):
            for l in range(k + 1, 8):
                q[k] = q[k] - m[k, l] * q[l]
        o = jnp.zeros((8, B), F32)
        for k in range(8):
            rk = row[k] * rs[k]
            for l in range(k + 1, 8):
                rk = jnp.where(lane == base + l, D[k, l] * rs[k], rk)
            o = jnp.where(sub == k, rk, o)
        out.append(o)
        for i in range(p + 1, 16):
            c = [lane_bcast(S[i], base + j) for j in range(8)]
            acc = jnp.where(inpanel, 0.0, S[i])
            if i == p + 1:
                for k in range(1, 8):
                    for j in range(k):
                        c[k] = c[k] - c[j] * m[j, k]
                for j in range(8):
                    acc = acc - c[j] * v[j]
            else:
                for j in range(8):
                    acc = acc - c[j] * q[j]
            S[i] = acc
    return out


def factor_kernel(scale, g_ref, r_ref, mh_ref, ml_ref, w_ref):
    n = r_ref.shape[0]
    nb = n // B
    for k, (i, j) in enumerate(tri_blocks(nb)):
        w_ref[i * B : (i + 1) * B, j * B : (j + 1) * B] = g_ref[k]
    li = lax.broadcasted_iota(jnp.int32, (B, B), 0)
    lj = lax.broadcasted_iota(jnp.int32, (B, B), 1)

    def dot(a, b):
        return jnp.dot(a, b, precision=HI, preferred_element_type=F32)

    def dot_t(a, b):
        return lax.dot_general(a, b, TT, precision=HI, preferred_element_type=F32)

    for b in range(nb):
        bs = slice(B * b, B * (b + 1))
        S = [w_ref[B * b + 8 * i : B * b + 8 * i + 8, bs] for i in range(16)]
        for i, o in enumerate(factor_block(S)):
            w_ref[B * b + 8 * i : B * b + 8 * i + 8, bs] = o
        F = w_ref[bs, bs]
        M = jnp.where(li >= lj, F, 0.0)
        before = slice(0, B * b)
        after = slice(B * (b + 1), n)
        if b > 0:
            w_ref[bs, before] = dot(M, w_ref[bs, before])
        if b < nb - 1:
            w_ref[bs, after] = dot(M, w_ref[bs, after])
        for i in range(b + 1, nb):
            s = slice(B * i, B * (i + 1))
            rest = slice(B * i, n)
            Rt = w_ref[bs, s]
            w_ref[s, rest] = w_ref[s, rest] - dot_t(Rt, w_ref[bs, rest])
            if b > 0:
                w_ref[s, before] = w_ref[s, before] - dot_t(Rt, w_ref[bs, before])
            w_ref[s, bs] = -dot_t(Rt, M)
        inv = 1.0 / scale
        R = jnp.where(li < lj, F, jnp.where(li == lj, 1.0 / F, 0.0))
        r_ref[bs, bs] = R * inv
        h, l = split(M * scale)
        mh_ref[bs, bs] = h
        ml_ref[bs, bs] = l
        if b > 0:
            r_ref[bs, before] = jnp.zeros((B, B * b), F32)
            h, l = split(w_ref[bs, before] * scale)
            mh_ref[bs, before] = h
            ml_ref[bs, before] = l
        if b < nb - 1:
            r_ref[bs, after] = w_ref[bs, after] * inv
            mh_ref[bs, after] = jnp.zeros((B, n - B * (b + 1)), BF16)
            ml_ref[bs, after] = jnp.zeros((B, n - B * (b + 1)), BF16)


def factor(gram, width, scale):
    vmem = pl.BlockSpec(memory_space=pltpu.VMEM)
    return pl.pallas_call(
        functools.partial(factor_kernel, scale),
        out_shape=(
            jax.ShapeDtypeStruct((width, width), F32),
            jax.ShapeDtypeStruct((width, width), BF16),
            jax.ShapeDtypeStruct((width, width), BF16),
        ),
        in_specs=[vmem],
        out_specs=(vmem, vmem, vmem),
        scratch_shapes=[pltpu.VMEM((width, width), F32)],
        compiler_params=pltpu.CompilerParams(vmem_limit_bytes=48 << 20),
        cost_estimate=pl.CostEstimate(
            flops=width**3, bytes_accessed=12 * width * width, transcendentals=0
        ),
        name="factor",
    )(gram)


def whiten_kernel(x_ref, mean_ref, mh_ref, ml_ref, o_ref):
    width = x_ref.shape[1]
    h, l = split(x_ref[...] - mean_ref[...])
    for j in range(0, width, 2 * B):
        top = j + 2 * B
        mh = mh_ref[j:top, :top]
        ml = ml_ref[j:top, :top]
        o = lax.dot_general(h[:, :top], ml, NT, preferred_element_type=F32)
        o += lax.dot_general(l[:, :top], mh, NT, preferred_element_type=F32)
        o += lax.dot_general(h[:, :top], mh, NT, preferred_element_type=F32)
        o_ref[:, j:top] = o


def whiten(x, mean, mh, ml):
    rows, width = x.shape
    step = rows // 6
    whole = lambda i: (0, 0)
    return pl.pallas_call(
        whiten_kernel,
        grid=(rows // step,),
        out_shape=jax.ShapeDtypeStruct((rows, width), F32),
        in_specs=[
            pl.BlockSpec((step, width), lambda i: (i, 0)),
            pl.BlockSpec((1, width), whole),
            pl.BlockSpec((width, width), whole),
            pl.BlockSpec((width, width), whole),
        ],
        out_specs=pl.BlockSpec((step, width), lambda i: (i, 0)),
        compiler_params=pltpu.CompilerParams(vmem_limit_bytes=48 << 20),
        cost_estimate=pl.CostEstimate(
            flops=2 * rows * width * width, bytes_accessed=8 * rows * width, transcendentals=0
        ),
        name="whiten",
    )(x, mean, mh, ml)


def shards(dims, row_count, embeddings):
    gram, mean = summed_gram(dims, embeddings)
    scale = math.sqrt(row_count)
    r, mh, ml = factor(gram, embeddings.shape[1], scale)
    return whiten(embeddings, mean, mh, ml), r


def solution(mesh):
    nx = mesh.shape["grp"]
    ny = 4
    nz = mesh.shape["wide"] // (2 * ny)

    def whole(embeddings):
        rows, width = embeddings.shape
        return jax.shard_map(
            functools.partial(shards, (nx, ny, nz, width), rows),
            mesh=mesh,
            in_specs=(P(("grp", "wide"), None),),
            out_specs=(P(("grp", "wide"), None), P()),
            check_vma=False,
        )(embeddings)

    return whole
```

time: 644 us -> 110 us (0.17); the launches traced: 636 us -> 110 us
  waiting for transfers between devices: 250 us -> 0 us
  other arithmetic: 197 us -> 0 us
  Pallas kernels: 0 us -> 107 us
  blocking collectives: 81.4 us -> 0 us
  matrix products: 57.9 us -> 0 us
  local copies, waits for them, and re-layouts: 31 us -> 1.99 us
  between operations: 18.5 us -> 0.65 us
    psum x1 -> x0, waiting for transfers between devices: 250 us -> none  [shards(): payload = lax.psum(self_product(centred), ('grp', 'wide'))]
    another operation x24 -> x0, other arithmetic: 183 us -> none  [the longest x22 124 us: shards(): lower = jnp.linalg.cholesky(payload)]
    pallas_call x0 -> x3, Pallas kernels: none -> 107 us  [the longest x1 67 us: summed_gram(): pl.pallas_call(functools.partial(gram_kernel, dims), out_shape=(jax.Shape...]
    psum x1 -> x0, blocking collectives: 81.4 us -> none  [shards(): col_total = lax.psum(jnp.sum(embeddings, axis=0), ('grp', 'wide'))]
    another operation x21 -> x0, matrix products: 41.6 us -> none  [the longest x11 31.8 us: shards(): solved = jax.scipy.linalg.solve_triangular(lower, centred.T, lower=True)]
    another operation x25 -> x0, local copies, waits for them, and re-layouts: 16.8 us -> none
    dot_general x1 -> x0, matrix products: 16.3 us -> none  [self_product(): lax.dot_general(rows, rows, (((0,), (0,)), ((), ())), precision=lax.Preci...]
    unnamed x10 -> x4, local copies, waits for them, and re-layouts: 10.6 us -> 1.99 us
  transfers between devices with their start and end apart: 1 -> 0, of which waited for: 1 -> 0; matrix products, arithmetic and copies ran while one was open for 1% -> 0% of each run, Pallas kernels for 0% -> 0%
where the time goes in v1:
time: 110 us
  Pallas kernels  107 us (97%)
  local copies, waits for them, and re-layouts  1.99 us (2%)
    pallas_call x1, Pallas kernels, summed_gram(): pl.pallas_call(functools.partial(gram_kernel, dims), out_shape=(jax.Shape...  67 us
    pallas_call x1, Pallas kernels, factor(): pl.pallas_call(functools.partial(factor_kernel, scale), out_shape=(jax.Sh...  31.7 us
    pallas_call x1, Pallas kernels, whiten(): pl.pallas_call(whiten_kernel, grid=(rows // step,), out_shape=jax.ShapeDt...  8.27 us

profile of v1, /device:TPU:1, one launch (start us, length us, event | category | flops | bytes accessed | tf_op | source)
XLA Modules:
  0.0 109.7 jit_solution(7311777061281711624)
XLA Ops:
  0.6 67.0 %summed_gram.1 = (f32[21,128,128]{2,1,0:T(8,128)}, f32[1,768]{1,0:T(1,128)}) custom-call(f32[1536,768]{1,0:T(8,128)} %x_ref.3), custom_call_target="tpu_custom_call" | custom-call | flops 1811939328 | bytes 4718592 | tf_op jit(solution)/shard_map/summed_gram/pallas_call | solution.py:276
  67.6 0.0 copy-start.1
  67.7 1.3 %copy-done.1 = f32[21,128,128]{2,1,0:T(8,128)S(1)} copy-done((f32[21,128,128]{2,1,0:T(8,128)S(1)}, f32[21,128,128]{2,1,0:T(8,128)}, u32[]{:S(2)}) %copy-start.1) | copy-done | bytes 1376280
  69.0 31.7 %factor.1 = (f32[768,768]{1,0:T(8,128)}, bf16[768,768]{1,0:T(8,128)(2,1)S(1)}, bf16[768,768]{1,0:T(8,128)(2,1)S(1)}) custom-call(f32[21,128,128]{2,1,0:T(8,128)S(1)} %copy-done.1), custom_call_target="tpu_custom_call" | custom-call | flops 452984832 | bytes 7077888 | tf_op jit(solution)/shard_map/factor/pallas_call | solution.py:425
  100.7 0.0 copy-start
  100.7 0.7 copy-done
  101.4 8.3 %whiten.1 = f32[1536,768]{1,0:T(8,128)} custom-call(f32[1536,768]{1,0:T(8,128)} %x_ref.3, f32[1,768]{1,0:T(1,128)S(1)} %copy-done, bf16[768,768]{1,0:T(8,128)(2,1)S(1)} %get-tuple-element.9.mh_ref, bf16[768,768]{1,0:T(8,128)(2,1)S(1)} %get-tuple-element.10.ml_ref), custom_call_target="tpu_custom_call" | custom-call | flops 1811939328 | bytes 9437184 | tf_op jit(solution)/shard_map/whiten/pallas_call | solution.py:460
Async XLA Ops:
  67.6 1.3 %copy-start.1 = (f32[21,128,128]{2,1,0:T(8,128)S(1)}, f32[21,128,128]{2,1,0:T(8,128)}, u32[]{:S(2)}) copy-start(f32[21,128,128]{2,1,0:T(8,128)} %get-tuple-element.8.g_ref) | copy-start | bytes 4128772
  100.7 0.7 copy-start

commit v2 on v1

v2 whole, which is shorter than its diff:
```python
import functools
import math

import jax
import jax.numpy as jnp
from jax import lax
from jax.experimental import pallas as pl
from jax.experimental.pallas import tpu as pltpu
from jax.sharding import PartitionSpec as P

F32 = jnp.float32
BF16 = jnp.bfloat16
HI = lax.Precision.HIGHEST
MESH = pl.DeviceIdType.MESH
B = 128
TT = (((0,), (0,)), ((), ()))
NT = (((1,), (1,)), ((), ()))


def tri_blocks(nb):
    return [
        (i, j)
        for pair in range(nb // 2 - 1, -1, -1)
        for j in (2 * pair, 2 * pair + 1)
        for i in range(j + 1)
    ]


def split(x):
    hi = x.astype(BF16)
    return hi, (x - hi.astype(F32)).astype(BF16)


def gram_kernel(
    dims,
    x_hbm,
    out_ref,
    mean_ref,
    xv,
    hi,
    lo,
    own,
    g_ref,
    bmat,
    from_core,
    a_in,
    b_own,
    b_in,
    z_own,
    z_in,
    z_all,
    b_all,
    mbuf,
    m_near,
    m_far,
    dm,
    ssem,
    rsem,
    xsem,
):
    nx, ny, nz, width = dims
    rows = xv.shape[0]
    nb = width // B
    blocks = tri_blocks(nb)
    at = {ij: k for k, ij in enumerate(blocks)}

    chunk = rows // 6
    x_copies = []
    for c in range(6):
        part = slice(c * chunk, (c + 1) * chunk)
        x_copies.append(pltpu.make_async_copy(x_hbm.at[part], xv.at[part], xsem.at[c]))
        x_copies[-1].start()

    mx = lax.axis_index("grp")
    wide = lax.axis_index("wide")
    mc = lax.rem(wide, 2)
    chip = wide // 2
    mz = lax.rem(chip, nz)
    my = chip // nz

    def dev(x, y, z, c):
        return (x, (y * nz + z) * 2 + c)

    def x_peer(d):
        return dev(lax.rem(mx + d, nx), my, mz, mc)

    def y_peer(d):
        return dev(mx, lax.rem(my + d, ny), mz, mc)

    def z_peer(d):
        return dev(mx, my, lax.rem(mz + d, nz), mc)

    core_peer = dev(mx, my, mz, 1 - mc)
    near = (
        [core_peer]
        + [x_peer(d) for d in range(1, nx)]
        + [dev(lax.rem(mx + d, nx), my, mz, 1 - mc) for d in range(1, nx)]
    )
    y_peers = [y_peer(d) for d in range(1, ny)]
    z_peers = [z_peer(d) for d in range(1, nz)]
    everyone = near + y_peers + z_peers
    barrier = pltpu.get_barrier_semaphore()
    for who in everyone:
        pl.semaphore_signal(barrier, inc=1, device_id=who, device_id_type=MESH)

    sent = []

    def send(src, dst, who):
        k = len(sent)
        copy = pltpu.make_async_remote_copy(
            src_ref=src,
            dst_ref=dst,
            send_sem=ssem.at[k],
            recv_sem=rsem.at[k],
            device_id=who,
            device_id_type=MESH,
        )
        copy.start()
        sent.append(copy)
        return copy

    total = jnp.zeros((1, width), F32)
    for c in range(6):
        x_copies[c].wait()
        total = total + jnp.sum(xv[c * chunk : (c + 1) * chunk, :], axis=0, keepdims=True)
    local = total * (1.0 / rows)
    mbuf[...] = jnp.zeros((8, B), F32)
    for i in range(nb):
        mbuf[i : i + 1, :] = local[:, i * B : (i + 1) * B]
    pl.semaphore_wait(barrier, len(everyone))

    slot = mx * 2 + mc
    near_copies = [send(mbuf, m_near.at[slot], who) for who in near]
    m_near[slot] = mbuf[...]

    for c in range(6):
        part = slice(c * chunk, (c + 1) * chunk)
        h, l = split(xv[part, :] - local)
        hi[part, :] = h
        lo[part, :] = l

    own_t = own.reshape(nx, 2, 2, -1, B)
    core_t = from_core.reshape(nx, 2, -1, B)
    ta = own_t.shape[3]
    g_t = g_ref.reshape(nx, 2, 2, ta, B)
    tb = b_in.shape[2]
    tz = z_in.shape[1]

    def near_mean():
        for copy in near_copies:
            copy.wait_recv()
        acc = m_near[0]
        for k in range(1, 2 * nx):
            acc = acc + m_near[k]
        return acc * (1.0 / (2 * nx))

    core_copies = {}
    far_copies = []
    done = 0
    for step in range(nb // 2):
        pair = nb // 2 - 1 - step
        top = 2 * B * (pair + 1)
        cols = slice(2 * B * pair, top)
        g = lax.dot_general(hi[:, :top], hi[:, cols], TT, preferred_element_type=F32)
        g += lax.dot_general(hi[:, :top], lo[:, cols], TT, preferred_element_type=F32)
        g += lax.dot_general(lo[:, :top], hi[:, cols], TT, preferred_element_type=F32)
        g += lax.dot_general(lo[:, :top], lo[:, cols], TT, preferred_element_type=F32)
        if step == 0:
            group = near_mean()
            m_far[mz, my] = group
            y_copies = [send(m_far.at[mz, my], m_far.at[mz, my], who) for who in y_peers]
            delta = mbuf[...] - group
            delta_t = delta.T * float(rows)
            col = [jnp.broadcast_to(delta_t[:, i : i + 1], (B, B)) for i in range(nb)]
        if step == 1:
            for copy in y_copies:
                copy.wait_recv()
            far_copies = [send(m_far.at[mz], m_far.at[mz], who) for who in z_peers]
        for j in (2 * pair, 2 * pair + 1):
            row = jnp.broadcast_to(delta[j : j + 1, :], (B, B))
            for i in range(j + 1):
                off = (j - 2 * pair) * B
                own[at[i, j]] = g[i * B : (i + 1) * B, off : off + B] + col[i] * row
        done += 4 * pair + 3
        for k in range(nx):
            for q in range(2):
                if (k, q) not in core_copies and (4 * k + 2 * q + 2) * ta <= done * B:
                    core_copies[k, q] = send(own_t.at[k, q, 1 - mc], core_t.at[k, q], core_peer)

    ax = [(x_peer, mx), (y_peer, my)]
    a_copies = [[], []]
    for c in core_copies.values():
        c.wait_recv()
    for d in list(range(1, nx)) + [0]:
        for q in range(2):
            peer, me = ax[q]
            k = lax.rem(me + d, nx)
            own_t[k, q, mc] = own_t[k, q, mc] + core_t[k, q]
            if d:
                a_copies[q].append(send(own_t.at[k, q, mc], a_in.at[q, d - 1], peer(d)))
    b_copies = [[], []]
    for q in range(2):
        me = ax[q][1]
        acc = own_t[me, q, mc]
        for d in range(1, nx):
            a_copies[q][d - 1].wait_recv()
            acc = acc + a_in[q, d - 1]
        b_own[q, 0:ta] = acc
        b_own[q, ta:] = jnp.zeros((b_own.shape[1] - ta, B), F32)
        peer, me = ax[1 - q]
        for d in range(1, ny):
            k = lax.rem(me + d, ny)
            b_copies[q].append(
                send(
                    b_own.at[q, pl.ds(pl.multiple_of(k * tb, 8), tb)],
                    b_in.at[q, d - 1],
                    peer(d),
                )
            )
    for q in range(2):
        me = ax[1 - q][1]
        acc = b_own[q, pl.ds(pl.multiple_of(me * tb, 8), tb)]
        for d in range(1, ny):
            b_copies[q][d - 1].wait_recv()
            acc = acc + b_in[q, d - 1]
        z_own[q * tb : (q + 1) * tb] = acc
    z_own[2 * tb :] = jnp.zeros((z_own.shape[0] - 2 * tb, B), F32)
    z_copies = []
    for d in range(1, nz):
        k = lax.rem(mz + d, nz)
        z_copies.append(
            send(z_own.at[pl.ds(pl.multiple_of(k * tz, 8), tz)], z_in.at[d - 1], z_peer(d))
        )

    for copy in far_copies:
        copy.wait_recv()
    m_groups = m_far.reshape(nz * ny, 8, B)
    for i in range(nb):
        rows_i = m_groups[:, i, :]
        mean_i = jnp.sum(rows_i, axis=0, keepdims=True) * (1.0 / (nz * ny))
        mean_ref[:, i * B : (i + 1) * B] = mean_i
        dm[:, i * B : (i + 1) * B] = rows_i - mean_i

    acc = z_own[pl.ds(pl.multiple_of(mz * tz, 8), tz)]
    for d in range(1, nz):
        z_copies[d - 1].wait_recv()
        acc = acc + z_in[d - 1]
    mine = pl.ds(pl.multiple_of(mz * tz, 8), tz)
    z_all[mine] = acc
    z_copies = [send(z_all.at[mine], z_all.at[mine], who) for who in z_peers]

    for pair in range(nb // 2):
        top = 2 * B * (pair + 1)
        g = lax.dot_general(
            dm[:, :top], dm[:, top - 2 * B : top], TT, precision=HI, preferred_element_type=F32
        ) * float(2 * nx * rows)
        for j in (2 * pair, 2 * pair + 1):
            for i in range(j + 1):
                off = (j - 2 * pair) * B
                bmat[at[i, j]] = g[i * B : (i + 1) * B, off : off + B]

    for c in z_copies:
        c.wait_recv()
    b_copies = [[], []]
    for q in range(2):
        peer, me = ax[1 - q]
        mine = pl.ds(pl.multiple_of(me * tb, 8), tb)
        src = z_all.at[q * tb : (q + 1) * tb]
        b_copies[q] = [send(src, b_all.at[q, mine], peer(d)) for d in range(1, ny)]
        b_all[q, mine] = z_all[q * tb : (q + 1) * tb]
    a_copies = [[], []]
    back = []
    for q in range(2):
        for c in b_copies[q]:
            c.wait_recv()
        peer, me = ax[q]
        src = b_all.at[q, 0:ta]
        a_copies[q] = [send(src, g_t.at[me, q, mc], peer(d)) for d in range(1, nx)]
        back.append(send(src, g_t.at[me, q, mc], core_peer))
        g_t[me, q, mc] = b_all[q, 0:ta]
    for d in range(1, nx):
        for q in range(2):
            a_copies[q][d - 1].wait_recv()
            k = lax.rem(ax[q][1] + nx - d, nx)
            back.append(send(g_t.at[k, q, mc], g_t.at[k, q, mc], core_peer))
    for c in back:
        c.wait_recv()
    for k in range(len(blocks)):
        out_ref[k] = g_ref[k] + bmat[k]
    for c in sent:
        c.wait_send()


def summed_gram(dims, x):
    nx, ny, nz, width = dims
    rows = x.shape[0]
    nb = width // B
    n_blocks = nb * (nb + 1) // 2
    total = n_blocks * B
    ta = total // (4 * nx)
    tb = -(-ta // (8 * ny)) * 8
    tz = -(-2 * tb // (8 * nz)) * 8
    n_mean = 2 * nx - 1 + (ny - 1) + (nz - 1)
    n_copies = n_mean + 2 * (2 * nx + 2 * (nx - 1) + 2 * (ny - 1) + nz - 1)
    vmem = pl.BlockSpec(memory_space=pltpu.VMEM)
    return pl.pallas_call(
        functools.partial(gram_kernel, dims),
        out_shape=(
            jax.ShapeDtypeStruct((n_blocks, B, B), F32),
            jax.ShapeDtypeStruct((1, width), F32),
        ),
        in_specs=[pl.BlockSpec(memory_space=pl.ANY)],
        out_specs=(vmem, vmem),
        scratch_shapes=[
            pltpu.VMEM((rows, width), F32),
            pltpu.VMEM((rows, width), BF16),
            pltpu.VMEM((rows, width), BF16),
            pltpu.VMEM((n_blocks, B, B), F32),
            pltpu.VMEM((n_blocks, B, B), F32),
            pltpu.VMEM((n_blocks, B, B), F32),
            pltpu.VMEM((total // 2, B), F32),
            pltpu.VMEM((2, nx - 1, ta, B), F32),
            pltpu.VMEM((2, tb * ny, B), F32),
            pltpu.VMEM((2, ny - 1, tb, B), F32),
            pltpu.VMEM((tz * nz, B), F32),
            pltpu.VMEM((nz - 1, tz, B), F32),
            pltpu.VMEM((tz * nz, B), F32),
            pltpu.VMEM((2, tb * ny, B), F32),
            pltpu.VMEM((8, B), F32),
            pltpu.VMEM((2 * nx, 8, B), F32),
            pltpu.VMEM((nz, ny, 8, B), F32),
            pltpu.VMEM((nz * ny, width), F32),
            pltpu.SemaphoreType.DMA((n_copies,)),
            pltpu.SemaphoreType.DMA((n_copies,)),
            pltpu.SemaphoreType.DMA((6,)),
        ],
        compiler_params=pltpu.CompilerParams(
            collective_id=0, has_side_effects=True, vmem_limit_bytes=56 << 20
        ),
        cost_estimate=pl.CostEstimate(
            flops=2 * rows * width * width, bytes_accessed=4 * rows * width, transcendentals=0
        ),
        name="summed_gram",
    )(x)


def rows_bcast(x, k):
    return jnp.broadcast_to(x[k : k + 1, :], (8, B))
def lane_bcast(x, c):
    return jnp.broadcast_to(x[:, c : c + 1], (8, B))


def factor_block(S, ones):
    lane = lax.broadcasted_iota(jnp.int32, (8, B), 1)
    sub = lax.broadcasted_iota(jnp.int32, (8, B), 0)
    S = list(S)
    out = []
    D = [lane_bcast(S[0], l) * ones for l in range(8)]
    for p in range(16):
        base = 8 * p
        inpanel = (lane >= base) & (lane < base + 8)
        C = D
        more = p < 15
        row_s = S[p]
        row_t = jnp.where(inpanel, jnp.where(lane == base + sub, 1.0, 0.0), S[p])
        if more:
            c = [lane_bcast(S[p + 1], base + j) * ones for j in range(8)]
            D = [lane_bcast(S[p + 1], base + 8 + l) * ones for l in range(8)]
            nxt = jnp.where(inpanel, 0.0, S[p + 1])
        pivot = rows_bcast(C[0], 0)
        diag = rdiag = None
        for j in range(8):
            r = 1.0 / pivot
            U = {l: rows_bcast(C[l], j) for l in range(j + 1, 8)}
            m = jnp.where(sub > j, C[j], 0.0) * r
            diag = pivot if j == 0 else jnp.where(sub == j, pivot, diag)
            rdiag = r if j == 0 else jnp.where(sub == j, r, rdiag)
            if j < 7:
                pivot = rows_bcast(C[j + 1], j + 1) - (U[j + 1] * U[j + 1]) * r
            for l in range(j + 1, 8):
                C[l] = C[l] - m * U[l]
            us = rows_bcast(row_s, j)
            ut = rows_bcast(row_t, j)
            row_s = row_s - m * us
            row_t = row_t - m * ut
            if more:
                e = c[j] * r
                for k in range(j + 1, 8):
                    c[k] = c[k] - e * U[k]
                for l in range(8):
                    D[l] = D[l] - e * rows_bcast(c[j], l)
                nxt = nxt - e * ut
        rs = lax.rsqrt(diag)
        out.append(jnp.where(lane > base + sub, row_s, row_t) * rs)
        if p < 14:
            Q = row_t * rdiag
            for l in range(7, 0, -1):
                Q = Q - (jnp.where(sub < l, C[l], 0.0) * rdiag) * rows_bcast(Q, l)
            q = [rows_bcast(Q, j) for j in range(8)]
            for i in range(p + 2, 16):
                acc = jnp.where(inpanel, 0.0, S[i])
                for j in range(8):
                    acc = acc - lane_bcast(S[i], base + j) * q[j]
                S[i] = acc
        if more:
            S[p + 1] = nxt
    return out

def factor_whiten_kernel(scale, g_ref, mean_ref, x_hbm, r_ref, o_hbm, w_ref, mh, ml, xv, hi, lo, o, xsem, osem, ones_ref):
    n = r_ref.shape[0]
    nb = n // B
    rows = xv.shape[0]
    CH = rows // 4
    xcopies = [pltpu.make_async_copy(x_hbm.at[c*CH:(c+1)*CH], xv.at[c*CH:(c+1)*CH], xsem.at[c]) for c in range(4)]
    for c in xcopies: c.start()
    for k, (i, j) in enumerate(tri_blocks(nb)):
        w_ref[i * B : (i + 1) * B, j * B : (j + 1) * B] = g_ref[k]
    li = lax.broadcasted_iota(jnp.int32, (B, B), 0)
    lj = lax.broadcasted_iota(jnp.int32, (B, B), 1)
    inv = 1.0 / scale

    def dot(a, b):
        return jnp.dot(a, b, precision=HI, preferred_element_type=F32)

    def dot_t(a, b):
        return lax.dot_general(a, b, TT, precision=HI, preferred_element_type=F32)

    def do_split(c):
        def f():
            if c % 4 == 0: xcopies[c // 4].wait()
            s = slice(c * CH // 4, (c + 1) * CH // 4)
            h, l = split(xv[s, :] - mean_ref[...])
            hi[s, :] = h
            lo[s, :] = l
        return f

    def do_whiten(b, c):
        def f():
            s = slice(c * CH, (c + 1) * CH)
            cs = slice(B * b, B * (b + 1))
            top = B * (b + 1)
            h = hi[s, :top]
            a = lax.dot_general(h, ml[cs, :top], NT, preferred_element_type=F32)
            a += lax.dot_general(lo[s, :top], mh[cs, :top], NT, preferred_element_type=F32)
            a += lax.dot_general(h, mh[cs, :top], NT, preferred_element_type=F32)
            o[s, cs] = a
        return f

    ocopies = []
    def out_copy(b):
        def f():
            cs = slice(B * b, B * (b + 1))
            cp = pltpu.make_async_copy(o.at[:, cs], o_hbm.at[:, cs], osem.at[b])
            cp.start()
            ocopies.append(cp)
        return f

    ones_ref[...] = jnp.full((8, B), 1.0, F32)
    ones = ones_ref[...]
    work = [do_split(c) for c in range(16)]
    for b in range(nb):
        bs = slice(B * b, B * (b + 1))
        S = [w_ref[B * b + 8 * i : B * b + 8 * i + 8, bs] for i in range(16)]
        for i, t in enumerate(factor_block(S, ones)):
            w_ref[B * b + 8 * i : B * b + 8 * i + 8, bs] = t
        for f in work:
            f()
        F = w_ref[bs, bs]
        M = jnp.where(li >= lj, F, 0.0)
        before = slice(0, B * b)
        after = slice(B * (b + 1), n)
        nxt = slice(B * (b + 1), B * (b + 2))
        beyond = slice(B * (b + 2), n)
        if b < nb - 1:
            Rn = dot(M, w_ref[bs, nxt])
            w_ref[bs, nxt] = Rn
            w_ref[nxt, nxt] = w_ref[nxt, nxt] - dot_t(Rn, Rn)
        work = []

        def finish_row(b=b, bs=bs, before=before, beyond=beyond, after=after, M=M, F=F):
            if b > 0:
                w_ref[bs, before] = dot(M, w_ref[bs, before])
            if b < nb - 2:
                w_ref[bs, beyond] = dot(M, w_ref[bs, beyond])

        def outputs(b=b, bs=bs, before=before, after=after, M=M, F=F):
            R = jnp.where(li < lj, F, jnp.where(li == lj, 1.0 / F, 0.0))
            r_ref[bs, bs] = R * inv
            h, l = split(M * scale)
            mh[bs, bs] = h
            ml[bs, bs] = l
            if b > 0:
                r_ref[bs, before] = jnp.zeros((B, B * b), F32)
                h, l = split(w_ref[bs, before] * scale)
                mh[bs, before] = h
                ml[bs, before] = l
            if b < nb - 1:
                r_ref[bs, after] = w_ref[bs, after] * inv

        def update_next(b=b, bs=bs, nxt=nxt, before=before, beyond=beyond, M=M):
            Rn = w_ref[bs, nxt]
            if b < nb - 2:
                w_ref[nxt, beyond] = w_ref[nxt, beyond] - dot_t(Rn, w_ref[bs, beyond])
            if b > 0:
                w_ref[nxt, before] = w_ref[nxt, before] - dot_t(Rn, w_ref[bs, before])
            w_ref[nxt, bs] = -dot_t(Rn, M)

        def update_beyond(b=b, bs=bs, before=before, beyond=beyond, M=M):
            Ra = w_ref[bs, beyond]
            w_ref[beyond, beyond] = w_ref[beyond, beyond] - dot_t(Ra, Ra)
            if b > 0:
                w_ref[beyond, before] = w_ref[beyond, before] - dot_t(Ra, w_ref[bs, before])
            w_ref[beyond, bs] = -dot_t(Ra, M)

        work.append(finish_row)
        work.append(outputs)
        if b < nb - 1:
            work.append(update_next)
        if b < nb - 2:
            work.append(update_beyond)
        work += [do_whiten(b, c) for c in range(4)]
        work.append(out_copy(b))
    for f in work:
        f()
    for c in ocopies:
        c.wait()

def factor_whiten(gram, mean, x, scale):
    rows, width = x.shape
    vmem = pl.BlockSpec(memory_space=pltpu.VMEM)
    hbm = pl.BlockSpec(memory_space=pl.ANY)
    return pl.pallas_call(
        functools.partial(factor_whiten_kernel, scale),
        out_shape=(
            jax.ShapeDtypeStruct((width, width), F32),
            jax.ShapeDtypeStruct((rows, width), F32),
        ),
        in_specs=[vmem, vmem, hbm],
        out_specs=(vmem, hbm),
        scratch_shapes=[pltpu.VMEM((width, width), F32), pltpu.VMEM((width, width), BF16), pltpu.VMEM((width, width), BF16),
            pltpu.VMEM((rows, width), F32), pltpu.VMEM((rows, width), BF16), pltpu.VMEM((rows, width), BF16), pltpu.VMEM((rows, width), F32),
            pltpu.SemaphoreType.DMA((4,)), pltpu.SemaphoreType.DMA((width // B,)), pltpu.VMEM((8, B), F32)],
        compiler_params=pltpu.CompilerParams(vmem_limit_bytes=56 << 20),
        name="factor_whiten",
    )(gram, mean, x)


def shards(dims, row_count, embeddings):
    gram, mean = summed_gram(dims, embeddings)
    r, whitened = factor_whiten(gram, mean, embeddings, math.sqrt(row_count))
    return whitened, r


def solution(mesh):
    nx = mesh.shape["grp"]
    ny = 4
    nz = mesh.shape["wide"] // (2 * ny)

    def whole(embeddings):
        rows, width = embeddings.shape
        return jax.shard_map(
            functools.partial(shards, (nx, ny, nz, width), rows),
            mesh=mesh,
            in_specs=(P(("grp", "wide"), None),),
            out_specs=(P(("grp", "wide"), None), P()),
            check_vma=False,
        )(embeddings)

    return whole
```

time: 110 us -> 86.7 us (0.79)
  Pallas kernels: 107 us -> 85.7 us
  local copies, waits for them, and re-layouts: 1.99 us -> 0 us
    pallas_call x2 -> x1, Pallas kernels: 40 us -> 26 us  [factor_whiten(): pl.pallas_call(functools.partial(factor_whiten_kernel, scale), out_shape=...]
    pallas_call x1, Pallas kernels: 67 us -> 59.7 us  [summed_gram(): pl.pallas_call(functools.partial(gram_kernel, dims), out_shape=(jax.Shape...]
    unnamed x4 -> x0, local copies, waits for them, and re-layouts: 1.99 us -> none
where the time goes in v2:
time: 86.7 us; the launch traced here: 86.6 us
  Pallas kernels  85.7 us (99%)
    pallas_call x1, Pallas kernels, summed_gram(): pl.pallas_call(functools.partial(gram_kernel, dims), out_shape=(jax.Shape...  59.7 us
    pallas_call x1, Pallas kernels, factor_whiten(): pl.pallas_call(functools.partial(factor_whiten_kernel, scale), out_shape=...  26 us

profile of v2, /device:TPU:1, one launch (start us, length us, event | category | flops | bytes accessed | tf_op | source)
XLA Modules:
  0.0 86.6 jit_solution(3682160334576805114)
XLA Ops:
  0.6 59.7 %summed_gram.1 = (f32[21,128,128]{2,1,0:T(8,128)}, f32[1,768]{1,0:T(1,128)}) custom-call(f32[1536,768]{1,0:T(8,128)} %x_hbm.3), custom_call_target="tpu_custom_call" | custom-call | flops 1811939328 | bytes 4718592 | tf_op jit(solution)/shard_map/summed_gram/pallas_call | solution.py:306
  60.4 26.0 %factor_whiten.1 = (f32[768,768]{1,0:T(8,128)}, f32[1536,768]{1,0:T(8,128)}) custom-call(f32[21,128,128]{2,1,0:T(8,128)} %get-tuple-element.6.g_ref, f32[1,768]{1,0:T(1,128)} %get-tuple-element.7.mean_ref, f32[1536,768]{1,0:T(8,128)} %x_hbm.3), custom_call_target="tpu_custom_call" | custom-call | tf_op jit(solution)/shard_map/factor_whiten/pallas_call | solution.py:532

commit v3 on v2

--- a/solution.py
+++ b/solution.py
@@ -17,13 +17,15 @@
 NT = (((1,), (1,)), ((), ()))
 
 
+def row_pairs(nb):
+    return [
+        [(i, j) for i in (2 * pair, 2 * pair + 1) for j in range(i, nb)]
+        for pair in range(nb // 2)
+    ]
+
+
 def tri_blocks(nb):
-    return [
-        (i, j)
-        for pair in range(nb // 2 - 1, -1, -1)
-        for j in (2 * pair, 2 * pair + 1)
-        for i in range(j + 1)
-    ]
+    return [ij for pair in row_pairs(nb) for ij in pair]
 
 
 def split(x):
@@ -39,11 +41,18 @@
     xv,
     hi,
     lo,
-    own,
-    g_ref,
+    own0,
+    own1,
+    own2,
+    core0,
+    core1,
+    core2,
+    a_in0,
+    a_in1,
+    a_in2,
+    head,
+    tail,
     bmat,
-    from_core,
-    a_in,
     b_own,
     b_in,
     z_own,
@@ -139,12 +148,17 @@
         hi[part, :] = h
         lo[part, :] = l
 
-    own_t = own.reshape(nx, 2, 2, -1, B)
-    core_t = from_core.reshape(nx, 2, -1, B)
-    ta = own_t.shape[3]
-    g_t = g_ref.reshape(nx, 2, 2, ta, B)
+    pairs = row_pairs(nb)
+    own = (own0, own1, own2)
+    core_in = (core0, core1, core2)
+    a_in = (a_in0, a_in1, a_in2)
+    part = [a.shape[2] for a in a_in]
+    first = [sum(part[:k]) for k in range(len(part))]
+    own_t = [o.reshape(2, 2, nx, n, B) for o, n in zip(own, part)]
+    ta = sum(part)
     tb = b_in.shape[2]
     tz = z_in.shape[1]
+    ax = [(x_peer, mx), (y_peer, my)]
 
     def near_mean():
         for copy in near_copies:
@@ -154,58 +168,54 @@
             acc = acc + m_near[k]
         return acc * (1.0 / (2 * nx))
 
-    core_copies = {}
-    far_copies = []
-    done = 0
-    for step in range(nb // 2):
-        pair = nb // 2 - 1 - step
-        top = 2 * B * (pair + 1)
-        cols = slice(2 * B * pair, top)
-        g = lax.dot_general(hi[:, :top], hi[:, cols], TT, preferred_element_type=F32)
-        g += lax.dot_general(hi[:, :top], lo[:, cols], TT, preferred_element_type=F32)
-        g += lax.dot_general(lo[:, :top], hi[:, cols], TT, preferred_element_type=F32)
-        g += lax.dot_general(lo[:, :top], lo[:, cols], TT, preferred_element_type=F32)
-        if step == 0:
+    core_copies = []
+    a_copies = []
+
+    def scatter_a(k):
+        core_copies[k].wait_recv()
+        own_t[k][mc] = own_t[k][mc] + core_in[k][...]
+        copies = [[], []]
+        for d in range(1, nx):
+            for q in range(2):
+                peer, me = ax[q]
+                to = lax.rem(me + d, nx)
+                copies[q].append(send(own_t[k].at[mc, q, to], a_in[k].at[q, d - 1], peer(d)))
+        a_copies.append(copies)
+
+    for k, pair in enumerate(pairs):
+        rs = slice(2 * B * k, 2 * B * (k + 1))
+        rest = slice(2 * B * k, width)
+        g = lax.dot_general(hi[:, rs], hi[:, rest], TT, preferred_element_type=F32)
+        g += lax.dot_general(hi[:, rs], lo[:, rest], TT, preferred_element_type=F32)
+        g += lax.dot_general(lo[:, rs], hi[:, rest], TT, preferred_element_type=F32)
+        if k == 0:
             group = near_mean()
             m_far[mz, my] = group
             y_copies = [send(m_far.at[mz, my], m_far.at[mz, my], who) for who in y_peers]
             delta = mbuf[...] - group
             delta_t = delta.T * float(rows)
-            col = [jnp.broadcast_to(delta_t[:, i : i + 1], (B, B)) for i in range(nb)]
-        if step == 1:
-            for copy in y_copies:
-                copy.wait_recv()
-            far_copies = [send(m_far.at[mz], m_far.at[mz], who) for who in z_peers]
-        for j in (2 * pair, 2 * pair + 1):
+        for n, (i, j) in enumerate(pair):
+            col = jnp.broadcast_to(delta_t[:, i : i + 1], (B, B))
             row = jnp.broadcast_to(delta[j : j + 1, :], (B, B))
-            for i in range(j + 1):
-                off = (j - 2 * pair) * B
-                own[at[i, j]] = g[i * B : (i + 1) * B, off : off + B] + col[i] * row
-        done += 4 * pair + 3
-        for k in range(nx):
-            for q in range(2):
-                if (k, q) not in core_copies and (4 * k + 2 * q + 2) * ta <= done * B:
-                    core_copies[k, q] = send(own_t.at[k, q, 1 - mc], core_t.at[k, q], core_peer)
-
-    ax = [(x_peer, mx), (y_peer, my)]
-    a_copies = [[], []]
-    for c in core_copies.values():
-        c.wait_recv()
-    for d in list(range(1, nx)) + [0]:
-        for q in range(2):
-            peer, me = ax[q]
-            k = lax.rem(me + d, nx)
-            own_t[k, q, mc] = own_t[k, q, mc] + core_t[k, q]
-            if d:
-                a_copies[q].append(send(own_t.at[k, q, mc], a_in.at[q, d - 1], peer(d)))
+            gi, gj = (i - 2 * k) * B, (j - 2 * k) * B
+            own[k][n] = g[gi : gi + B, gj : gj + B] + col * row
+        core_copies.append(send(own_t[k].at[1 - mc], core_in[k], core_peer))
+        if k:
+            scatter_a(k - 1)
+    for copy in y_copies:
+        copy.wait_recv()
+    far_copies = [send(m_far.at[mz], m_far.at[mz], who) for who in z_peers]
+    scatter_a(len(pairs) - 1)
+
     b_copies = [[], []]
     for q in range(2):
         me = ax[q][1]
-        acc = own_t[me, q, mc]
-        for d in range(1, nx):
-            a_copies[q][d - 1].wait_recv()
-            acc = acc + a_in[q, d - 1]
-        b_own[q, 0:ta] = acc
+        for k in range(len(pairs)):
+            acc = own_t[k][mc, q, me]
+            for d in range(1, nx):
+                a_copies[k][q][d - 1].wait_recv()
+                acc = acc + a_in[k][q, d - 1]
+            b_own[q, first[k] : first[k] + part[k]] = acc
         b_own[q, ta:] = jnp.zeros((b_own.shape[1] - ta, B), F32)
         peer, me = ax[1 - q]
         for d in range(1, ny):
@@ -249,15 +259,15 @@
     z_all[mine] = acc
     z_copies = [send(z_all.at[mine], z_all.at[mine], who) for who in z_peers]
 
-    for pair in range(nb // 2):
-        top = 2 * B * (pair + 1)
+    for k, pair in enumerate(pairs):
+        rs = slice(2 * B * k, 2 * B * (k + 1))
+        rest = slice(2 * B * k, width)
         g = lax.dot_general(
-            dm[:, :top], dm[:, top - 2 * B : top], TT, precision=HI, preferred_element_type=F32
+            dm[:, rs], dm[:, rest], TT, precision=HI, preferred_element_type=F32
         ) * float(2 * nx * rows)
-        for j in (2 * pair, 2 * pair + 1):
-            for i in range(j + 1):
-                off = (j - 2 * pair) * B
-                bmat[at[i, j]] = g[i * B : (i + 1) * B, off : off + B]
+        for i, j in pair:
+            gi, gj = (i - 2 * k) * B, (j - 2 * k) * B
+            bmat[at[i, j]] = g[gi : gi + B, gj : gj + B]
 
     for c in z_copies:
         c.wait_recv()
@@ -268,25 +278,43 @@
         src = z_all.at[q * tb : (q + 1) * tb]
         b_copies[q] = [send(src, b_all.at[q, mine], peer(d)) for d in range(1, ny)]
         b_all[q, mine] = z_all[q * tb : (q + 1) * tb]
-    a_copies = [[], []]
     back = []
-    for q in range(2):
-        for c in b_copies[q]:
-            c.wait_recv()
-        peer, me = ax[q]
-        src = b_all.at[q, 0:ta]
-        a_copies[q] = [send(src, g_t.at[me, q, mc], peer(d)) for d in range(1, nx)]
-        back.append(send(src, g_t.at[me, q, mc], core_peer))
-        g_t[me, q, mc] = b_all[q, 0:ta]
-    for d in range(1, nx):
+    gathers = []
+    for dst, at_row, n in ((head, 0, part[0]), (tail, part[0], ta - part[0])):
+        copies = [[], []]
         for q in range(2):
-            a_copies[q][d - 1].wait_recv()
-            k = lax.rem(ax[q][1] + nx - d, nx)
-            back.append(send(g_t.at[k, q, mc], g_t.at[k, q, mc], core_peer))
+            if dst is head:
+                for c in b_copies[q]:
+                    c.wait_recv()
+            peer, me = ax[q]
+            src = b_all.at[q, at_row : at_row + n]
+            copies[q] = [send(src, dst.at[mc, q, me], peer(d)) for d in range(1, nx)]
+            back.append(send(src, dst.at[mc, q, me], core_peer))
+            dst[mc, q, me] = b_all[q, at_row : at_row + n]
+        gathers.append(copies)
+    for dst, copies in zip((head, tail), gathers):
+        for d in range(1, nx):
+            for q in range(2):
+                copies[q][d - 1].wait_recv()
+                k = lax.rem(ax[q][1] + nx - d, nx)
+                back.append(send(dst.at[mc, q, k], dst.at[mc, q, k], core_peer))
     for c in back:
         c.wait_recv()
-    for k in range(len(blocks)):
-        out_ref[k] = g_ref[k] + bmat[k]
+    n_head = len(pairs[0])
+    whole_head = head.reshape(n_head, B, B)
+    for k in range(n_head):
+        out_ref[k] = whole_head[k] + bmat[k]
+    pieces = tail.reshape(4 * nx, ta - part[0], B)
+    start = n_head
+    for k in range(1, len(pairs)):
+        for t in range(len(pairs[k]) * B // 8):
+            piece, off = divmod(8 * t, part[k])
+            off += first[k] - part[0]
+            block, row = start + 8 * t // B, 8 * t % B
+            out_ref[block, row : row + 8] = (
+                pieces[piece, off : off + 8] + bmat[block, row : row + 8]
+            )
+        start += len(pairs[k])
     for c in sent:
         c.wait_send()
 
@@ -296,12 +324,13 @@
     rows = x.shape[0]
     nb = width // B
     n_blocks = nb * (nb + 1) // 2
-    total = n_blocks * B
-    ta = total // (4 * nx)
+    sizes = [len(pair) for pair in row_pairs(nb)]
+    part = [n * B // (4 * nx) for n in sizes]
+    ta = sum(part)
     tb = -(-ta // (8 * ny)) * 8
     tz = -(-2 * tb // (8 * nz)) * 8
     n_mean = 2 * nx - 1 + (ny - 1) + (nz - 1)
-    n_copies = n_mean + 2 * (2 * nx + 2 * (nx - 1) + 2 * (ny - 1) + nz - 1)
+    n_copies = n_mean + 3 + 6 * (nx - 1) + 4 * (ny - 1) + 2 * (nz - 1) + 4 * (nx - 1) + 4 * nx
     vmem = pl.BlockSpec(memory_space=pltpu.VMEM)
     return pl.pallas_call(
         functools.partial(gram_kernel, dims),
@@ -315,11 +344,12 @@
             pltpu.VMEM((rows, width), F32),
             pltpu.VMEM((rows, width), BF16),
             pltpu.VMEM((rows, width), BF16),
+            *[pltpu.VMEM((n, B, B), F32) for n in sizes],
+            *[pltpu.VMEM((2, nx, n, B), F32) for n in part],
+            *[pltpu.VMEM((2, nx - 1, n, B), F32) for n in part],
+            pltpu.VMEM((2, 2, nx, part[0], B), F32),
+            pltpu.VMEM((2, 2, nx, ta - part[0], B), F32),
             pltpu.VMEM((n_blocks, B, B), F32),
-            pltpu.VMEM((n_blocks, B, B), F32),
-            pltpu.VMEM((n_blocks, B, B), F32),
-            pltpu.VMEM((total // 2, B), F32),
-            pltpu.VMEM((2, nx - 1, ta, B), F32),
             pltpu.VMEM((2, tb * ny, B), F32),
             pltpu.VMEM((2, ny - 1, tb, B), F32),
             pltpu.VMEM((tz * nz, B), F32),

time: 86.7 us -> 81.4 us (0.939)
  Pallas kernels: 85.7 us -> 80.5 us
    pallas_call x1, Pallas kernels: 59.7 us -> 54.5 us  [summed_gram(): pl.pallas_call(functools.partial(gram_kernel, dims), out_shape=(jax.Shape...]
where the time goes in v3:
time: 81.4 us; the launch traced here: 81.3 us
  Pallas kernels  80.5 us (99%)
  between operations  0.82 us (1%)
    pallas_call x1, Pallas kernels, summed_gram(): pl.pallas_call(functools.partial(gram_kernel, dims), out_shape=(jax.Shape...  54.5 us
    pallas_call x1, Pallas kernels, factor_whiten(): pl.pallas_call(functools.partial(factor_whiten_kernel, scale), out_shape=...  26 us

profile of v3, /device:TPU:1, one launch (start us, length us, event | category | flops | bytes accessed | tf_op | source)
XLA Modules:
  0.0 81.3 jit_solution(4680827040207037083)
XLA Ops:
  0.6 54.5 %summed_gram.1 = (f32[21,128,128]{2,1,0:T(8,128)}, f32[1,768]{1,0:T(1,128)}) custom-call(f32[1536,768]{1,0:T(8,128)} %x_hbm.3), custom_call_target="tpu_custom_call" | custom-call | flops 1811939328 | bytes 4718592 | tf_op jit(solution)/shard_map/summed_gram/pallas_call | solution.py:335
  55.1 26.0 %factor_whiten.1 = (f32[768,768]{1,0:T(8,128)}, f32[1536,768]{1,0:T(8,128)}) custom-call(f32[21,128,128]{2,1,0:T(8,128)} %get-tuple-element.6.g_ref, f32[1,768]{1,0:T(1,128)} %get-tuple-element.7.mean_ref, f32[1536,768]{1,0:T(8,128)} %x_hbm.3), custom_call_target="tpu_custom_call" | custom-call | tf_op jit(solution)/shard_map/factor_whiten/pallas_call | solution.py:562

commit v4 on v3

--- a/solution.py
+++ b/solution.py
@@ -436,7 +436,7 @@
             S[p + 1] = nxt
     return out
 
-def factor_whiten_kernel(scale, g_ref, mean_ref, x_hbm, r_ref, o_hbm, w_ref, mh, ml, xv, hi, lo, o, xsem, osem, ones_ref):
+def factor_whiten_kernel(scale, g_ref, mean_ref, x_hbm, r_hbm, o_hbm, r_ref, w_ref, mh, ml, xv, hi, lo, o, xsem, osem, rsem, ones_ref):
     n = r_ref.shape[0]
     nb = n // B
     rows = xv.shape[0]
@@ -464,27 +464,23 @@
             lo[s, :] = l
         return f
 
-    def do_whiten(b, c):
+    def do_whiten(pair, c):
         def f():
             s = slice(c * CH, (c + 1) * CH)
-            cs = slice(B * b, B * (b + 1))
-            top = B * (b + 1)
+            top = 2 * B * (pair + 1)
+            cs = slice(top - 2 * B, top)
             h = hi[s, :top]
             a = lax.dot_general(h, ml[cs, :top], NT, preferred_element_type=F32)
             a += lax.dot_general(lo[s, :top], mh[cs, :top], NT, preferred_element_type=F32)
             a += lax.dot_general(h, mh[cs, :top], NT, preferred_element_type=F32)
             o[s, cs] = a
-        return f
-
-    ocopies = []
-    def out_copy(b):
-        def f():
-            cs = slice(B * b, B * (b + 1))
-            cp = pltpu.make_async_copy(o.at[:, cs], o_hbm.at[:, cs], osem.at[b])
+            cp = pltpu.make_async_copy(o.at[s, cs], o_hbm.at[s, cs], osem.at[4 * pair + c])
             cp.start()
             ocopies.append(cp)
+
         return f
 
+    ocopies = []
     ones_ref[...] = jnp.full((8, B), 1.0, F32)
     ones = ones_ref[...]
     work = [do_split(c) for c in range(16)]
@@ -513,7 +509,7 @@
             if b < nb - 2:
                 w_ref[bs, beyond] = dot(M, w_ref[bs, beyond])
 
-        def outputs(b=b, bs=bs, before=before, after=after, M=M, F=F):
+        def outputs(b=b, bs=bs, nxt=nxt, before=before, after=after, M=M, F=F):
             R = jnp.where(li < lj, F, jnp.where(li == lj, 1.0 / F, 0.0))
             r_ref[bs, bs] = R * inv
             h, l = split(M * scale)
@@ -526,6 +522,13 @@
                 ml[bs, before] = l
             if b < nb - 1:
                 r_ref[bs, after] = w_ref[bs, after] * inv
+            if b % 2 == 0:
+                none = jnp.zeros((B, B), BF16)
+                mh[bs, nxt] = none
+                ml[bs, nxt] = none
+            cp = pltpu.make_async_copy(r_ref.at[bs, :], r_hbm.at[bs, :], rsem.at[b])
+            cp.start()
+            ocopies.append(cp)
 
         def update_next(b=b, bs=bs, nxt=nxt, before=before, beyond=beyond, M=M):
             Rn = w_ref[bs, nxt]
@@ -548,8 +551,8 @@
             work.append(update_next)
         if b < nb - 2:
             work.append(update_beyond)
-        work += [do_whiten(b, c) for c in range(4)]
-        work.append(out_copy(b))
+        if b % 2:
+            work += [do_whiten(b // 2, c) for c in range(4)]
     for f in work:
         f()
     for c in ocopies:
@@ -566,10 +569,10 @@
             jax.ShapeDtypeStruct((rows, width), F32),
         ),
         in_specs=[vmem, vmem, hbm],
-        out_specs=(vmem, hbm),
-        scratch_shapes=[pltpu.VMEM((width, width), F32), pltpu.VMEM((width, width), BF16), pltpu.VMEM((width, width), BF16),
+        out_specs=(hbm, hbm),
+        scratch_shapes=[pltpu.VMEM((width, width), F32), pltpu.VMEM((width, width), F32), pltpu.VMEM((width, width), BF16), pltpu.VMEM((width, width), BF16),
             pltpu.VMEM((rows, width), F32), pltpu.VMEM((rows, width), BF16), pltpu.VMEM((rows, width), BF16), pltpu.VMEM((rows, width), F32),
-            pltpu.SemaphoreType.DMA((4,)), pltpu.SemaphoreType.DMA((width // B,)), pltpu.VMEM((8, B), F32)],
+            pltpu.SemaphoreType.DMA((4,)), pltpu.SemaphoreType.DMA((2 * width // B,)), pltpu.SemaphoreType.DMA((width // B,)), pltpu.VMEM((8, B), F32)],
         compiler_params=pltpu.CompilerParams(vmem_limit_bytes=56 << 20),
         name="factor_whiten",
     )(gram, mean, x)

time: 81.4 us -> 80.3 us (0.986)
  Pallas kernels: 80.5 us -> 79.4 us
    pallas_call x1, Pallas kernels: 26 us -> 24.9 us  [factor_whiten(): pl.pallas_call(functools.partial(factor_whiten_kernel, scale), out_shape=...]
where the time goes in v4:
time: 80.3 us; the launch traced here: 80.2 us
  Pallas kernels  79.4 us (99%)
  between operations  0.82 us (1%)
    pallas_call x1, Pallas kernels, summed_gram(): pl.pallas_call(functools.partial(gram_kernel, dims), out_shape=(jax.Shape...  54.5 us
    pallas_call x1, Pallas kernels, factor_whiten(): pl.pallas_call(functools.partial(factor_whiten_kernel, scale), out_shape=...  24.9 us

profile of v4, /device:TPU:1, one launch (start us, length us, event | category | flops | bytes accessed | tf_op | source)
XLA Modules:
  0.0 80.2 jit_solution(2493727915699889133)
XLA Ops:
  0.6 54.5 %summed_gram.1 = (f32[21,128,128]{2,1,0:T(8,128)}, f32[1,768]{1,0:T(1,128)}) custom-call(f32[1536,768]{1,0:T(8,128)} %x_hbm.3), custom_call_target="tpu_custom_call" | custom-call | flops 1811939328 | bytes 4718592 | tf_op jit(solution)/shard_map/summed_gram/pallas_call | solution.py:335
  55.1 24.9 %factor_whiten.1 = (f32[768,768]{1,0:T(8,128)}, f32[1536,768]{1,0:T(8,128)}) custom-call(f32[21,128,128]{2,1,0:T(8,128)} %get-tuple-element.6.g_ref, f32[1,768]{1,0:T(1,128)} %get-tuple-element.7.mean_ref, f32[1536,768]{1,0:T(8,128)} %x_hbm.3), custom_call_target="tpu_custom_call" | custom-call | tf_op jit(solution)/shard_map/factor_whiten/pallas_call | solution.py:565
